TPU v7x, 768 devices: a whole 4x8x12 slice. The times are simulated.
768 devices in a mesh: dp: 96 (over y, z), fsdp: 8 (over x, core).
Axes of the slice: x: 4, y: 8, z: 12, core: 2. Of those that a mesh axis runs over, the one named last changes fastest.
Arguments:
- tokens: bfloat16 [98304, 4096], P(('dp', 'fsdp')), may hold values from -6 to 6
- value_grad: bfloat16 [98304, 1024], P(('dp', 'fsdp')), may hold values from -6 to 6
- value_weight: bfloat16 [4096, 1024], P('fsdp'), may hold values from -0.1875 to 0.1875
- counts: int32 [768], P(('dp', 'fsdp')), may hold values from 66 to 88, as said below
- chosen_rows: int32 [768, 88], P(('dp', 'fsdp')), may hold values from 0 to 127, as said below
- loss_scale: float32 [1], replicated, may hold values from 129.98462 to 519.9385
Outputs:
- grad_tokens: bfloat16 [98304, 4096], P(('dp', 'fsdp'))
- grad_weight: float32 [4096, 1024], P('fsdp')
Inputs may be any that keep to these rules, and one draw needn't show every extreme that they name: `counts`: each device's count lies between 66 and 88; some device has exactly 88, a different one in different draws. `chosen_rows`: the 88 entries of a device's row are distinct row numbers of that device.
All inputs are finite; a program needn't handle non-finite values.
Results may differ from a plain program's by a relative error of at most 0.001.
Values may be sent and summed in bfloat16 or wider, within the bound.
A program may use at most 32 MiB of HBM per device.

v0:
```python
import jax
import jax.numpy as jnp
from jax import lax
from jax.sharding import PartitionSpec as P


def shards(tokens, value_grad, value_weight, counts, chosen_rows, loss_scale):
    chosen = chosen_rows[0]
    slots = lax.broadcasted_iota(jnp.int32, (chosen.shape[0], 1), 0)
    live_mask = slots < counts[0]
    picked = tokens[chosen]
    cotangent = jnp.where(live_mask, value_grad[chosen], jnp.zeros((), jnp.bfloat16))
    width = value_weight.shape[0]
    every_rows, every_grad = (
        lax.all_gather(picked, "fsdp", axis=0, tiled=True),
        lax.all_gather(cotangent, "fsdp", axis=0, tiled=True),
    )
    column_part = lax.dynamic_slice_in_dim(every_rows, lax.axis_index("fsdp") * width, width, 1)
    partial_grad = lax.dot_general(
        column_part, every_grad, (((0,), (0,)), ((), ())), preferred_element_type=jnp.float32
    )
    summed = lax.psum(partial_grad, "dp")
    grad_weight = summed / loss_scale[0]
    input_part = lax.dot_general(
        every_grad, value_weight, (((1,), (1,)), ((), ())), preferred_element_type=jnp.float32
    ).astype(jnp.bfloat16)
    own_grad = lax.all_to_all(input_part, "fsdp", split_axis=0, concat_axis=1, tiled=True)
    grad_tokens = jnp.zeros(tokens.shape, jnp.bfloat16).at[chosen].set(own_grad)
    return (grad_tokens, grad_weight)


def solution(mesh):
    return jax.shard_map(
        shards,
        mesh=mesh,
        in_specs=(
            P(("dp", "fsdp"), None),
            P(("dp", "fsdp"), None),
            P("fsdp", None),
            P(("dp", "fsdp")),
            P(("dp", "fsdp"), None),
            P(),
        ),
        out_specs=(P(("dp", "fsdp"), None), P("fsdp", None)),
        check_vma=False,
    )
```

profile of v0, /device:TPU:6, one launch (start us, length us, event | category | flops | bytes accessed | tf_op | source)
XLA Modules:
  0.0 354.7 jit_solution(17981176232966151264)
XLA Ops:
  7.2 0.0 copy-start
  7.2 0.0 all-gather.4.cloned.1.call-start
  7.2 0.7 fusion.4
  8.6 1.9 gather_fusion
  10.5 0.8 broadcast_select_fusion
  11.3 0.0 all-gather.4.cloned.1.call-update
  11.3 0.0 all-gather.6.cloned.1.call-start
  11.3 0.0 copy-done
  11.4 1.8 gather_fusion.1
  13.2 0.0 all-gather.6.cloned.1.call-update
  13.2 0.0 all-reduce.2.cloned.1.call-start
  13.3 36.0 %all-gather.4.cloned.1.call-done = bf16[704,1024]{1,0:T(8,128)(2,1)} async-done(((bf16[88,1024]{1,0:T(8,128)(2,1)}), bf16[704,1024]{1,0:T(8,128)(2,1)}) %all-gather.4.cloned.1.call-update) | async-done | bytes 1441808 | tf_op jit(solution)/shard_map/all_gather | solution.py:16
  49.3 49.3 %all-gather.6.cloned.1.call-done = bf16[704,4096]{1,0:T(8,128)(2,1)} async-done(((bf16[88,4096]{1,0:T(8,128)(2,1)}), bf16[704,4096]{1,0:T(8,128)(2,1)}) %all-gather.6.cloned.1.call-update) | async-done | bytes 5767184 | tf_op jit(solution)/shard_map/all_gather | solution.py:15
  98.6 0.0 copy-start.2
  98.6 4.0 %fusion = f32[512,1024]{1,0:T(8,128)} fusion(bf16[704,1024]{1,0:T(8,128)(2,1)} %all-gather.4.cloned.1.call-done, bf16[704,4096]{1,0:T(8,128)(2,1)} %all-gather.6.cloned.1.call-done, s32[]{:T(128)S(6)} %select_n.21), kind=kOutput, calls=%fused_computation.5 | convolution fusion | flops 738197504 | bytes 4259844 | tf_op jit(solution)/shard_map/dot_general | solution.py:19
  102.6 0.0 copy-start.1
  102.6 0.0 all-reduce.2.cloned.1.call-update
  102.6 0.0 copy-done.2
  102.6 1.3 copy-done.1
  104.0 1.8 convolution_convert_fusion
  105.8 5.9 %all-to-all-start = ((bf16[8,88,512]{2,1,0:T(8,128)(2,1)}), bf16[8,88,512]{2,1,0:T(8,128)(2,1)S(1)}, u32[]{:S(2)}, u32[]{:S(2)}) async-start(bf16[8,88,512]{2,1,0:T(8,128)(2,1)} %bitcast.3), calls=%async_computation | async-start | bytes 1441792 | tf_op jit(solution)/shard_map/all_to_all | solution.py:27
  112.3 9.7 %all-to-all-done = bf16[8,88,512]{2,1,0:T(8,128)(2,1)S(1)} async-done(((bf16[8,88,512]{2,1,0:T(8,128)(2,1)}), bf16[8,88,512]{2,1,0:T(8,128)(2,1)S(1)}, u32[]{:S(2)}, u32[]{:S(2)}) %all-to-all-start) | async-done | bytes 720928 | tf_op jit(solution)/shard_map/all_to_all | solution.py:27
  122.0 0.1 copy.10
  122.1 2.6 scatter_custom_fusion
  124.7 220.2 %all-reduce.2.cloned.1.call-done = f32[512,1024]{1,0:T(8,128)} async-done(((f32[512,1024]{1,0:T(8,128)}), f32[512,1024]{1,0:T(8,128)}) %all-reduce.2.cloned.1.call-update) | async-done | bytes 2097168 | tf_op jit(solution)/shard_map/psum | solution.py:22
  344.9 3.2 broadcast_divide_fusion
  (2 shorter events, 0.0 us)
Async XLA Ops:
  7.2 4.2 %copy-start = (bf16[128,4096]{1,0:T(8,128)(2,1)S(1)}, bf16[128,4096]{1,0:T(8,128)(2,1)}, u32[]{:S(2)}) copy-start(bf16[128,4096]{1,0:T(8,128)(2,1)} %param.6) | copy-start | bytes 3145732
  7.2 42.1 %all-gather.4.cloned.1.call-start = ((), (), s32[]{:S(2)}) async-start(), calls=%async_computation.1 | async-start | bytes 1622016 | tf_op jit(solution)/shard_map/all_gather | solution.py:16
  11.3 87.3 %all-gather.6.cloned.1.call-start = ((), (), s32[]{:S(2)}) async-start(), calls=%async_computation.3 | async-start | bytes 6488064 | tf_op jit(solution)/shard_map/all_gather | solution.py:15
  13.2 331.7 %all-reduce.2.cloned.1.call-start = ((), (), s32[]{:S(2)}) async-start(), calls=%async_computation.2 | async-start | bytes 4194304 | tf_op jit(solution)/shard_map/psum | solution.py:22
  98.6 4.0 %copy-start.2 = (bf16[512,1024]{1,0:T(8,128)(2,1)S(1)}, bf16[512,1024]{1,0:T(8,128)(2,1)}, u32[]{:S(2)}) copy-start(bf16[512,1024]{1,0:T(8,128)(2,1)} %param.8) | copy-start | bytes 3145732
  102.6 1.4 copy-start.1
  105.8 16.2 %all-to-all-start = ((bf16[8,88,512]{2,1,0:T(8,128)(2,1)}), bf16[8,88,512]{2,1,0:T(8,128)(2,1)S(1)}, u32[]{:S(2)}, u32[]{:S(2)}) async-start(bf16[8,88,512]{2,1,0:T(8,128)(2,1)} %bitcast.3), calls=%async_computation | async-start | bytes 1441792 | tf_op jit(solution)/shard_map/all_to_all | solution.py:27
Sparse Core Ops, SparseCore 0:
  11.4 37.8 all-gather.3
  52.3 46.2 all-gather.5
  102.9 241.9 all-reduce.1
where the time goes:
time: 355 us
  waiting for transfers between devices  315 us (89%)
  between operations  15.1 us (4%)
  local copies, waits for them, and re-layouts  7.76 us (2%)
  starting transfers between devices  5.99 us (2%)
  matrix products  5.79 us (2%)
  other arithmetic  4.71 us (1%)
    psum x1, waiting for transfers between devices, shards(): summed = lax.psum(partial_grad, 'dp')  220 us
    all_gather x1, waiting for transfers between devices, shards(): lax.all_gather(picked, 'fsdp', axis=0, tiled=True)  49.3 us
    all_gather x1, waiting for transfers between devices, shards(): lax.all_gather(cotangent, 'fsdp', axis=0, tiled=True)  36 us
    all_to_all x1, waiting for transfers between devices, shards(): lax.all_to_all(input_part, 'fsdp', split_axis=0, concat_axis=1, tiled=True)  9.71 us
  transfers between devices with their start and end apart: 4, of which 4 were waited for; matrix products, arithmetic and copies ran while one was open for 2% of the time, Pallas kernels for 0%

commit v1 on v0

v1 whole, which is shorter than its diff:
```python
import jax
import jax.numpy as jnp
from jax import lax
from jax.experimental import pallas as pl
from jax.experimental.pallas import tpu as pltpu
from jax.sharding import PartitionSpec as P

MESH = pl.DeviceIdType.MESH
NY, NZ, NF = 8, 12, 8
SLOTS = 96
ROWS, D, KV = 128, 4096, 1024
W = D // NF
CH = 4
CW = W // CH
ZR = 48
LANE = KV // NY
LONG, SHORT = NY // 2, NY // 2 - 1
f32, bf16 = jnp.float32, jnp.bfloat16


def dot(a, b, ca, cb):
    return lax.dot_general(a, b, (((ca,), (cb,)), ((), ())), preferred_element_type=f32)


def kernel(
    tok, vg, wt, sel, scale, gt_out, gw_out,
    picked, cots, parts, slot, own, gt, part, rl, rs, red, zrecv, zsum, full,
    cot_s, cot_r, sib_s, sib_r, pk_s, pk_r, sg_s, sg_r,
    l_s, l_r, s_s, s_r, z_s, z_r, az_s, az_r, al_s, al_r, as_s, as_r, out_s,
):
    dp, fs = lax.axis_index("dp"), lax.axis_index("fsdp")
    y, z = dp // NZ, lax.rem(dp, NZ)
    c, x = lax.rem(fs, 2), fs // 2
    sgn = 1 - 2 * c
    sib = x * 2 + 1 - c

    def at_y(v):
        return lax.rem(v + 2 * NY, NY)

    y_up, y_dn = at_y(y + sgn) * NZ + z, at_y(y - sgn) * NZ + z

    def zdev(d):
        return lax.rem(z + d, NZ)

    def fdev(d):
        return lax.rem(fs + d, NF)

    def xdev(d):
        return lax.rem(x + d, 4) * 2 + c

    def rcopy(src, dst, ss, rs_, dev):
        return pltpu.make_async_remote_copy(
            src_ref=src, dst_ref=dst, send_sem=ss, recv_sem=rs_, device_id=dev, device_id_type=MESH
        )

    barrier = pltpu.get_barrier_semaphore()
    peers = [(dp, fdev(d)) for d in range(1, NF)]
    peers += [(y_up, fs), (y_dn, fs)]
    peers += [(y * NZ + zdev(d), fs) for d in range(1, NZ)]
    for peer in peers:
        pl.semaphore_signal(barrier, inc=1, device_id=peer, device_id_type=MESH)

    rows = lax.broadcasted_iota(jnp.int32, (ROWS, ROWS), 0)
    hot = jnp.where(rows == sel[0:1, :], 1.0, 0.0).astype(bf16)
    cots[fs] = dot(hot, vg[...], 0, 0)[:SLOTS].astype(bf16)
    pl.semaphore_wait(barrier, len(peers))

    sends = []

    def go(cp):
        cp.start()
        sends.append(cp)

    for d in (1, 3, 2):
        go(rcopy(cots.at[fs], cots.at[fs], cot_s.at[d - 1], cot_r.at[d - 1], (dp, xdev(d))))
    go(rcopy(cots.at[fs], cots.at[fs], sib_s.at[0], sib_r.at[0], (dp, sib)))

    for b in range(4):
        cols = slice(b * 1024, (b + 1) * 1024)
        picked[:, cols] = dot(hot, tok[:, cols], 0, 0)[:SLOTS].astype(bf16)
    for k in range(CH):
        for d in (2, 6, 3, 7, 4, 5, 1):
            to = fdev(d)
            cols = pl.ds(pl.multiple_of(to * W + k * CW, CW), CW)
            go(rcopy(picked.at[:, cols], parts.at[k, fs], pk_s.at[k, d - 1], pk_r.at[k, d - 1], (dp, to)))
        cols = pl.ds(pl.multiple_of(fs * W + k * CW, CW), CW)
        parts[k, fs] = picked[:, cols]

    for d in (1, 3, 2):
        frm = xdev(4 - d)
        rcopy(cots.at[frm], cots.at[frm], cot_s.at[d - 1], cot_r.at[d - 1], (dp, frm)).wait_recv()
        go(rcopy(cots.at[frm], cots.at[frm], sib_s.at[d], sib_r.at[d], (dp, sib)))
    for d in range(4):
        frm = lax.rem(x + 4 - d, 4) * 2 + 1 - c
        rcopy(cots.at[frm], cots.at[frm], sib_s.at[d], sib_r.at[d], (dp, sib)).wait_recv()

    def long_copy(k, s):
        j = at_y(y - sgn * (LONG - s))
        src = part.at[j, pl.ds(k * CW, CW)] if s == 0 else rl.at[k, s - 1]
        return rcopy(src, rl.at[k, s], l_s.at[k, s], l_r.at[k, s], (y_dn, fs))

    def short_copy(k, s):
        j = at_y(y + sgn * (SHORT - s))
        src = part.at[j, pl.ds(k * CW, CW)] if s == 0 else rs.at[k, s - 1]
        return rcopy(src, rs.at[k, s], s_s.at[k, s], s_r.at[k, s], (y_up, fs))

    def product(k):
        for d in range(1, NF):
            frm = fdev(NF - d)
            rcopy(parts.at[k, frm], parts.at[k, frm], pk_s.at[k, d - 1], pk_r.at[k, d - 1], (dp, frm)).wait_recv()
        a = parts[k].reshape(NF * SLOTS, CW)
        b = cots[...].reshape(NF * SLOTS, KV)
        p = dot(a, b, 0, 0)
        for j in range(NY):
            part[j, k * CW:(k + 1) * CW] = p[:, j * LANE:(j + 1) * LANE]
        go(long_copy(k, 0))
        go(short_copy(k, 0))

    def ring_step(k, s):
        here = pl.ds(k * CW, CW)
        long_copy(k, s - 1).wait_recv()
        if s < LONG:
            rl[k, s - 1] += part[at_y(y - sgn * (LONG - s)), here]
            go(long_copy(k, s))
        if s <= SHORT:
            short_copy(k, s - 1).wait_recv()
        if s < SHORT:
            rs[k, s - 1] += part[at_y(y + sgn * (SHORT - s)), here]
            go(short_copy(k, s))
        if s == LONG:
            red[here] = part[y, here] + rl[k, LONG - 1] + rs[k, SHORT - 1]

    red[W:] = jnp.zeros((NZ * ZR - W, LANE), f32)

    def slot_grads():
        for g in range(2):
            b = cots[g * 4:(g + 1) * 4].reshape(4 * SLOTS, KV)
            q = dot(b, wt[...], 1, 1).astype(bf16)
            slot[g * 4:(g + 1) * 4] = q.reshape(4, SLOTS, W)
        for d in (2, 6, 3, 7, 4, 5, 1):
            to = fdev(d)
            go(rcopy(slot.at[to], own.at[fs], sg_s.at[d - 1], sg_r.at[d - 1], (dp, to)))
        own[fs] = slot[fs]

    product(0)
    slot_grads()
    for t in range(1, CH + LONG):
        if t < CH:
            product(t)
        for s in range(min(t, LONG), 0, -1):
            k = t - s
            if k < CH:
                ring_step(k, s)

    for d in (6, 5, 7, 4, 8, 3, 9, 2, 10, 1, 11):
        to = zdev(d)
        src = red.at[pl.ds(pl.multiple_of(to * ZR, 16), ZR)]
        go(rcopy(src, zrecv.at[d - 1], z_s.at[d - 1], z_r.at[d - 1], (y * NZ + to, fs)))

    for d in range(1, NF):
        frm = fdev(NF - d)
        rcopy(own.at[frm], own.at[frm], sg_s.at[d - 1], sg_r.at[d - 1], (dp, frm)).wait_recv()
    hot_s = hot[:, :SLOTS]
    for f in range(NF):
        gt[:, f * W:(f + 1) * W] = dot(hot_s, own[f], 1, 0).astype(bf16)
    gt_copy = pltpu.make_async_copy(gt, gt_out, out_s.at[NY])
    gt_copy.start()

    total = red[pl.ds(pl.multiple_of(z * ZR, 16), ZR)]
    for d in range(1, NZ):
        rcopy(zrecv.at[d - 1], zrecv.at[d - 1], z_s.at[d - 1], z_r.at[d - 1], (dp, fs)).wait_recv()
        total += zrecv[d - 1]
    zsum[...] = total / scale[0]

    mine = full.at[y, pl.ds(pl.multiple_of(z * ZR, 16), ZR)]
    for d in (6, 5, 7, 4, 8, 3, 9, 2, 10, 1, 11):
        go(rcopy(zsum, mine, az_s.at[d - 1], az_r.at[d - 1], (y * NZ + zdev(d), fs)))
    mine[...] = zsum[...]
    for d in range(1, NZ):
        there = full.at[y, pl.ds(pl.multiple_of(zdev(NZ - d) * ZR, 16), ZR)]
        rcopy(zsum, there, az_s.at[d - 1], az_r.at[d - 1], (dp, fs)).wait_recv()

    outs = []

    def put(j, i):
        cp = pltpu.make_async_copy(
            full.at[j, pl.ds(0, W)],
            gw_out.at[:, pl.ds(pl.multiple_of(j * LANE, LANE), LANE)], out_s.at[i]
        )
        cp.start()
        outs.append(cp)

    half = W // 2

    def along(s, h, up):
        j = at_y(y - sgn * s) if up else at_y(y + sgn * s)
        ref = full.at[j, pl.ds(h * half, half)]
        if up:
            return rcopy(ref, ref, al_s.at[s, h], al_r.at[s, h], (y_up, fs))
        return rcopy(ref, ref, as_s.at[s, h], as_r.at[s, h], (y_dn, fs))

    def arrived(s, h, up):
        j = at_y(y - sgn * (s + 1)) if up else at_y(y + sgn * (s + 1))
        ref = full.at[j, pl.ds(h * half, half)]
        sems = (al_s.at[s, h], al_r.at[s, h]) if up else (as_s.at[s, h], as_r.at[s, h])
        rcopy(ref, ref, *sems, (dp, fs)).wait_recv()
        return j

    for h in range(2):
        go(along(0, h, True))
        go(along(0, h, False))
    put(y, 0)
    for s in range(1, LONG + 1):
        for h in range(2):
            j = arrived(s - 1, h, True)
            if s < LONG:
                go(along(s, h, True))
            if s <= SHORT:
                i = arrived(s - 1, h, False)
                if s < SHORT:
                    go(along(s, h, False))
        put(j, s)
        if s <= SHORT:
            put(i, LONG + s)

    for cp in sends:
        cp.wait_send()
    for cp in outs:
        cp.wait()
    gt_copy.wait()


def shards(tokens, value_grad, value_weight, counts, chosen_rows, loss_scale):
    n = chosen_rows.shape[1]
    live = lax.broadcasted_iota(jnp.int32, (1, n), 1) < counts[0]
    sel = jnp.pad(jnp.where(live, chosen_rows, -1), ((0, 7), (0, ROWS - n)), constant_values=-1)
    vmem = pl.BlockSpec(memory_space=pltpu.VMEM)
    dma = pltpu.SemaphoreType.DMA
    scratch = [
        pltpu.VMEM((SLOTS, D), bf16),
        pltpu.VMEM((NF, SLOTS, KV), bf16),
        pltpu.VMEM((CH, NF, SLOTS, CW), bf16),
        pltpu.VMEM((NF, SLOTS, W), bf16),
        pltpu.VMEM((NF, SLOTS, W), bf16),
        pltpu.VMEM((ROWS, D), bf16),
        pltpu.VMEM((NY, W, LANE), f32),
        pltpu.VMEM((CH, LONG, CW, LANE), f32),
        pltpu.VMEM((CH, SHORT, CW, LANE), f32),
        pltpu.VMEM((NZ * ZR, LANE), f32),
        pltpu.VMEM((NZ - 1, ZR, LANE), f32),
        pltpu.VMEM((ZR, LANE), f32),
        pltpu.VMEM((NY, NZ * ZR, LANE), f32),
        dma((3,)), dma((3,)), dma((4,)), dma((4,)),
        dma((CH, NF - 1)), dma((CH, NF - 1)), dma((NF - 1,)), dma((NF - 1,)),
        dma((CH, LONG)), dma((CH, LONG)), dma((CH, SHORT)), dma((CH, SHORT)),
        dma((NZ - 1,)), dma((NZ - 1,)), dma((NZ - 1,)), dma((NZ - 1,)),
        dma((LONG, 2)), dma((LONG, 2)), dma((SHORT, 2)), dma((SHORT, 2)),
        dma((NY + 1,)),
    ]
    return pl.pallas_call(
        kernel,
        out_shape=(
            jax.ShapeDtypeStruct((ROWS, D), bf16),
            jax.ShapeDtypeStruct((W, KV), f32),
        ),
        in_specs=[vmem] * 4 + [pl.BlockSpec(memory_space=pltpu.SMEM)],
        out_specs=(pl.BlockSpec(memory_space=pl.ANY), pl.BlockSpec(memory_space=pl.ANY)),
        scratch_shapes=scratch,
        compiler_params=pltpu.CompilerParams(
            collective_id=0, has_side_effects=True, vmem_limit_bytes=48 << 20
        ),
    )(tokens, value_grad, value_weight, sel, loss_scale)


def solution(mesh):
    return jax.shard_map(
        shards,
        mesh=mesh,
        in_specs=(
            P(("dp", "fsdp"), None),
            P(("dp", "fsdp"), None),
            P("fsdp", None),
            P(("dp", "fsdp")),
            P(("dp", "fsdp"), None),
            P(),
        ),
        out_specs=(P(("dp", "fsdp"), None), P("fsdp", None)),
        check_vma=False,
    )
```

time: 355 us -> 115 us (0.32)
  waiting for transfers between devices: 315 us -> 0 us
  Pallas kernels: 0 us -> 104 us
  between operations: 15.1 us -> 1.93 us
  starting transfers between devices: 5.99 us -> 0 us
  matrix products: 5.79 us -> 0 us
  other arithmetic: 4.71 us -> 0.66 us
    psum x1 -> x0, waiting for transfers between devices: 220 us -> none  [shards(): summed = lax.psum(partial_grad, 'dp')]
    pallas_call x0 -> x1, Pallas kernels: none -> 104 us  [shards(): pl.pallas_call(kernel, out_shape=(jax.ShapeDtypeStruct((ROWS, D), bf16),...]
    all_gather x2 -> x0, waiting for transfers between devices: 85.3 us -> none  [the longest x1 49.3 us: shards(): lax.all_gather(picked, 'fsdp', axis=0, tiled=True)]
    all_to_all x1 -> x0, waiting for transfers between devices: 9.71 us -> none  [shards(): lax.all_to_all(input_part, 'fsdp', split_axis=0, concat_axis=1, tiled=True)]
    all_to_all x1 -> x0, starting transfers between devices: 5.87 us -> none  [shards(): lax.all_to_all(input_part, 'fsdp', split_axis=0, concat_axis=1, tiled=True)]
    dot_general x2 -> x0, matrix products: 5.79 us -> none  [the longest x1 3.99 us: shards(): lax.dot_general(column_part, every_grad, (((0,), (0,)), ((), ())), prefer...]
    unnamed x6 -> x8, local copies, waits for them, and re-layouts: 1.34 us -> 5.69 us
    gather x2 -> x0, local copies, waits for them, and re-layouts: 3.72 us -> none  [the longest x1 1.87 us: shards(): value_grad[chosen]]
  transfers between devices with their start and end apart: 4 -> 0, of which waited for: 4 -> 0; matrix products, arithmetic and copies ran while one was open for 2% -> 0% of each run, Pallas kernels for 0% -> 0%
where the time goes in v1:
time: 115 us; the launch traced here: 113 us
  Pallas kernels  104 us (90%)
  local copies, waits for them, and re-layouts  5.7 us (5%)
  between operations  1.93 us (2%)
    pallas_call x1, Pallas kernels, shards(): pl.pallas_call(kernel, out_shape=(jax.ShapeDtypeStruct((ROWS, D), bf16),...  104 us
    unnamed x8, local copies, waits for them, and re-layouts  5.69 us

profile of v1, /device:TPU:6, one launch (start us, length us, event | category | flops | bytes accessed | tf_op | source)
XLA Modules:
  0.0 112.7 jit_solution(16179264694094917503)
XLA Ops:
  1.9 0.7 compare_select_fusion
  2.6 0.0 copy-start
  2.6 1.2 %copy-done = bf16[128,4096]{1,0:T(8,128)(2,1)S(1)} copy-done((bf16[128,4096]{1,0:T(8,128)(2,1)S(1)}, bf16[128,4096]{1,0:T(8,128)(2,1)}, u32[]{:S(2)}) %copy-start) | copy-done | bytes 1048600
  3.8 0.0 copy-start.1
  3.8 1.2 %copy-done.1 = bf16[512,1024]{1,0:T(8,128)(2,1)S(1)} copy-done((bf16[512,1024]{1,0:T(8,128)(2,1)S(1)}, bf16[512,1024]{1,0:T(8,128)(2,1)}, u32[]{:S(2)}) %copy-start.1) | copy-done | bytes 1048600
  5.0 0.0 copy-start.2
  5.0 0.9 copy-done.2
  6.0 104.5 %shard_map.77 = (bf16[128,4096]{1,0:T(8,128)(2,1)S(1)}, f32[512,1024]{1,0:T(8,128)S(1)}) custom-call(bf16[128,4096]{1,0:T(8,128)(2,1)S(1)} %copy-done, bf16[128,1024]{1,0:T(8,128)(2,1)S(1)} %copy-done.2, bf16[512,1024]{1,0:T(8,128)(2,1)S(1)} %copy-done.1, s32[8,128]{1,0:T(8,128)S(1)} %pad.4.sel, f32[1]{0:T(128)S(6)} %copy.11.scale), custom_call_target="tpu_custom_call" | custom-call | tf_op jit(solution)/shard_map/pallas_call | solution.py:260
  110.5 1.0 copy.12
  111.4 1.3 %copy.13 = f32[512,1024]{1,0:T(8,128)} copy(f32[512,1024]{1,0:T(8,128)S(1)} %get-tuple-element.5) | data formatting | bytes 4194304
  (1 shorter events, 0.0 us)
Async XLA Ops:
  2.6 1.2 %copy-start = (bf16[128,4096]{1,0:T(8,128)(2,1)S(1)}, bf16[128,4096]{1,0:T(8,128)(2,1)}, u32[]{:S(2)}) copy-start(bf16[128,4096]{1,0:T(8,128)(2,1)} %tok.1) | copy-start | bytes 3145732
  3.8 1.2 %copy-start.1 = (bf16[512,1024]{1,0:T(8,128)(2,1)S(1)}, bf16[512,1024]{1,0:T(8,128)(2,1)}, u32[]{:S(2)}) copy-start(bf16[512,1024]{1,0:T(8,128)(2,1)} %wt.1) | copy-start | bytes 3145732
  5.0 0.9 copy-start.2

commit v2 on v1

--- a/solution.py
+++ b/solution.py
@@ -16,6 +16,7 @@
 LANE = KV // NY
 LONG, SHORT = NY // 2, NY // 2 - 1
 f32, bf16 = jnp.float32, jnp.bfloat16
+TOP, LOW = 2.0 ** 15.4, 2.0 ** -15.4
 
 
 def dot(a, b, ca, cb):
@@ -23,10 +24,10 @@
 
 
 def kernel(
-    tok, vg, wt, sel, scale, gt_out, gw_out,
-    picked, cots, parts, slot, own, gt, part, rl, rs, red, zrecv, zsum, full,
-    cot_s, cot_r, sib_s, sib_r, pk_s, pk_r, sg_s, sg_r,
-    l_s, l_r, s_s, s_r, z_s, z_r, az_s, az_r, al_s, al_r, as_s, as_r, out_s,
+    tok_in, vg_in, wt_in, count, chosen, scale, gt_out, gw_out,
+    tok, vg, wt, sel, picked, cots, parts, slot, own, part, el, es, rl, rs, red, ered, zrecv, zsum, full, xb, yb, zb,
+    gt, gw, in_s, out_s, xb_s, xb_r, yb_s, yb_r, zb_s, zb_r, cot_s, cot_r, sib_s, sib_r, pk_s, pk_r, sg_s, sg_r,
+    l_s, l_r, s_s, s_r, z_s, z_r, az_s, az_r, al_s, al_r, as_s, as_r,
 ):
     dp, fs = lax.axis_index("dp"), lax.axis_index("fsdp")
     y, z = dp // NZ, lax.rem(dp, NZ)
@@ -37,10 +38,17 @@
     def at_y(v):
         return lax.rem(v + 2 * NY, NY)
 
+    ins = [pltpu.make_async_copy(a, b, in_s.at[i]) for i, (a, b) in enumerate(((vg_in, vg), (tok_in, tok), (wt_in, wt)))]
+    for cp in ins:
+        cp.start()
+
     y_up, y_dn = at_y(y + sgn) * NZ + z, at_y(y - sgn) * NZ + z
 
     def zdev(d):
         return lax.rem(z + d, NZ)
+
+    def ydev(d):
+        return at_y(y + d) * NZ + z
 
     def fdev(d):
         return lax.rem(fs + d, NF)
@@ -55,14 +63,34 @@
 
     barrier = pltpu.get_barrier_semaphore()
     peers = [(dp, fdev(d)) for d in range(1, NF)]
-    peers += [(y_up, fs), (y_dn, fs)]
+    peers += [(ydev(d), fs) for d in range(1, NY)]
     peers += [(y * NZ + zdev(d), fs) for d in range(1, NZ)]
     for peer in peers:
         pl.semaphore_signal(barrier, inc=1, device_id=peer, device_id_type=MESH)
 
+    n = chosen.shape[1]
+    sel[...] = jnp.full(sel.shape, -1, jnp.int32)
+    live = lax.broadcasted_iota(jnp.int32, (1, n), 1) < count[0]
+    sel[0:1, 0:n] = jnp.where(live, chosen[...], -1)
     rows = lax.broadcasted_iota(jnp.int32, (ROWS, ROWS), 0)
     hot = jnp.where(rows == sel[0:1, :], 1.0, 0.0).astype(bf16)
-    cots[fs] = dot(hot, vg[...], 0, 0)[:SLOTS].astype(bf16)
+
+    def widest(v):
+        t = jnp.sum(v * v, axis=0, keepdims=True)
+        return jnp.max(t, axis=1, keepdims=True)
+
+    ins[0].wait()
+    v = dot(hot, vg[...], 0, 0)[:SLOTS]
+    cots[fs] = v.astype(bf16)
+    g_sq = widest(v)
+    ins[1].wait()
+    t_sq = jnp.zeros((1, 1), f32)
+    for b in range(4):
+        cols = slice(b * 1024, (b + 1) * 1024)
+        v = dot(hot, tok[:, cols], 0, 0)[:SLOTS]
+        picked[:, cols] = v.astype(bf16)
+        t_sq = jnp.maximum(t_sq, widest(v))
+    xb[0] = jnp.broadcast_to(jnp.sqrt(t_sq) * jnp.sqrt(g_sq), xb.shape[1:])
     pl.semaphore_wait(barrier, len(peers))
 
     sends = []
@@ -71,13 +99,23 @@
         cp.start()
         sends.append(cp)
 
+    def bounds(buf, ss, rs_, devs):
+        for d, dev in enumerate(devs):
+            go(rcopy(buf.at[0], buf.at[d + 1], ss.at[d], rs_.at[d], dev))
+
+    def largest(buf, ss, rs_):
+        top = buf[0]
+        for d in range(buf.shape[0] - 1):
+            rcopy(buf.at[d + 1], buf.at[d + 1], ss.at[d], rs_.at[d], (dp, fs)).wait_recv()
+            top = jnp.maximum(top, buf[d + 1])
+        return top
+
+    bounds(xb, xb_s, xb_r, [(dp, fdev(d)) for d in range(1, NF)])
+
     for d in (1, 3, 2):
         go(rcopy(cots.at[fs], cots.at[fs], cot_s.at[d - 1], cot_r.at[d - 1], (dp, xdev(d))))
     go(rcopy(cots.at[fs], cots.at[fs], sib_s.at[0], sib_r.at[0], (dp, sib)))
 
-    for b in range(4):
-        cols = slice(b * 1024, (b + 1) * 1024)
-        picked[:, cols] = dot(hot, tok[:, cols], 0, 0)[:SLOTS].astype(bf16)
     for k in range(CH):
         for d in (2, 6, 3, 7, 4, 5, 1):
             to = fdev(d)
@@ -86,6 +124,9 @@
         cols = pl.ds(pl.multiple_of(fs * W + k * CW, CW), CW)
         parts[k, fs] = picked[:, cols]
 
+    yb[0] = largest(xb, xb_s, xb_r)
+    bounds(yb, yb_s, yb_r, [(ydev(d), fs) for d in range(1, NY)])
+
     for d in (1, 3, 2):
         frm = xdev(4 - d)
         rcopy(cots.at[frm], cots.at[frm], cot_s.at[d - 1], cot_r.at[d - 1], (dp, frm)).wait_recv()
@@ -94,14 +135,34 @@
         frm = lax.rem(x + 4 - d, 4) * 2 + 1 - c
         rcopy(cots.at[frm], cots.at[frm], sib_s.at[d], sib_r.at[d], (dp, sib)).wait_recv()
 
+    def steps(bound):
+        a = TOP / jnp.maximum(bound[0:1], 1e-30)
+        return a, 1.0 / a
+
+    def code(v, a):
+        w = LOW + a * jnp.abs(v)
+        w = w * w
+        w = w * w
+        w = w * w
+        return jnp.where(v < 0, -w, w).astype(bf16)
+
+    def value(e, i):
+        e = e.astype(f32)
+        r = lax.rsqrt(lax.rsqrt(jnp.abs(e)))
+        w = (r * lax.rsqrt(r) - LOW) * i
+        return jnp.where(e < 0, -w, w)
+
+    zb[0] = largest(yb, yb_s, yb_r)
+    bounds(zb, zb_s, zb_r, [(y * NZ + zdev(d), fs) for d in range(1, NZ)])
+    y_a, y_i = steps(zb[0] * (NF * NY))
+    z_a = z_i = None
+
     def long_copy(k, s):
-        j = at_y(y - sgn * (LONG - s))
-        src = part.at[j, pl.ds(k * CW, CW)] if s == 0 else rl.at[k, s - 1]
+        src = el.at[k, s]
         return rcopy(src, rl.at[k, s], l_s.at[k, s], l_r.at[k, s], (y_dn, fs))
 
     def short_copy(k, s):
-        j = at_y(y + sgn * (SHORT - s))
-        src = part.at[j, pl.ds(k * CW, CW)] if s == 0 else rs.at[k, s - 1]
+        src = es.at[k, s]
         return rcopy(src, rs.at[k, s], s_s.at[k, s], s_r.at[k, s], (y_up, fs))
 
     def product(k):
@@ -113,24 +174,30 @@
         p = dot(a, b, 0, 0)
         for j in range(NY):
             part[j, k * CW:(k + 1) * CW] = p[:, j * LANE:(j + 1) * LANE]
+        here = pl.ds(k * CW, CW)
+        el[k, 0] = code(part[at_y(y - sgn * LONG), here], y_a)
         go(long_copy(k, 0))
+        es[k, 0] = code(part[at_y(y + sgn * SHORT), here], y_a)
         go(short_copy(k, 0))
 
     def ring_step(k, s):
         here = pl.ds(k * CW, CW)
         long_copy(k, s - 1).wait_recv()
         if s < LONG:
-            rl[k, s - 1] += part[at_y(y - sgn * (LONG - s)), here]
+            el[k, s] = code(part[at_y(y - sgn * (LONG - s)), here] + value(rl[k, s - 1], y_i), y_a)
             go(long_copy(k, s))
         if s <= SHORT:
             short_copy(k, s - 1).wait_recv()
         if s < SHORT:
-            rs[k, s - 1] += part[at_y(y + sgn * (SHORT - s)), here]
+            es[k, s] = code(part[at_y(y + sgn * (SHORT - s)), here] + value(rs[k, s - 1], y_i), y_a)
             go(short_copy(k, s))
         if s == LONG:
-            red[here] = part[y, here] + rl[k, LONG - 1] + rs[k, SHORT - 1]
+            total = part[y, here] + value(rl[k, LONG - 1], y_i) + value(rs[k, SHORT - 1], y_i)
+            red[here] = total
+            ered[here] = code(total, z_a)
 
     red[W:] = jnp.zeros((NZ * ZR - W, LANE), f32)
+    ered[W:] = jnp.zeros((NZ * ZR - W, LANE), bf16)
 
     def slot_grads():
         for g in range(2):
@@ -143,7 +210,9 @@
         own[fs] = slot[fs]
 
     product(0)
+    ins[2].wait()
     slot_grads()
+    z_a, z_i = steps(largest(zb, zb_s, zb_r) * (NF * NY * NZ))
     for t in range(1, CH + LONG):
         if t < CH:
             product(t)
@@ -154,7 +223,7 @@
 
     for d in (6, 5, 7, 4, 8, 3, 9, 2, 10, 1, 11):
         to = zdev(d)
-        src = red.at[pl.ds(pl.multiple_of(to * ZR, 16), ZR)]
+        src = ered.at[pl.ds(pl.multiple_of(to * ZR, 16), ZR)]
         go(rcopy(src, zrecv.at[d - 1], z_s.at[d - 1], z_r.at[d - 1], (y * NZ + to, fs)))
 
     for d in range(1, NF):
@@ -163,14 +232,14 @@
     hot_s = hot[:, :SLOTS]
     for f in range(NF):
         gt[:, f * W:(f + 1) * W] = dot(hot_s, own[f], 1, 0).astype(bf16)
-    gt_copy = pltpu.make_async_copy(gt, gt_out, out_s.at[NY])
-    gt_copy.start()
-
+
+    outs = [pltpu.make_async_copy(gt, gt_out, out_s.at[NY])]
+    outs[0].start()
     total = red[pl.ds(pl.multiple_of(z * ZR, 16), ZR)]
     for d in range(1, NZ):
         rcopy(zrecv.at[d - 1], zrecv.at[d - 1], z_s.at[d - 1], z_r.at[d - 1], (dp, fs)).wait_recv()
-        total += zrecv[d - 1]
-    zsum[...] = total / scale[0]
+        total += value(zrecv[d - 1], z_i)
+    zsum[...] = code(total, z_a)
 
     mine = full.at[y, pl.ds(pl.multiple_of(z * ZR, 16), ZR)]
     for d in (6, 5, 7, 4, 8, 3, 9, 2, 10, 1, 11):
@@ -180,13 +249,12 @@
         there = full.at[y, pl.ds(pl.multiple_of(zdev(NZ - d) * ZR, 16), ZR)]
         rcopy(zsum, there, az_s.at[d - 1], az_r.at[d - 1], (dp, fs)).wait_recv()
 
-    outs = []
-
-    def put(j, i):
-        cp = pltpu.make_async_copy(
-            full.at[j, pl.ds(0, W)],
-            gw_out.at[:, pl.ds(pl.multiple_of(j * LANE, LANE), LANE)], out_s.at[i]
-        )
+    out_i = z_i / scale[0]
+
+    def put(j):
+        i = len(outs) - 1
+        gw[i] = value(full[j, 0:W], out_i)
+        cp = pltpu.make_async_copy(gw.at[i], gw_out.at[:, pl.ds(pl.multiple_of(j * LANE, LANE), LANE)], out_s.at[i])
         cp.start()
         outs.append(cp)
 
@@ -209,7 +277,7 @@
     for h in range(2):
         go(along(0, h, True))
         go(along(0, h, False))
-    put(y, 0)
+    put(y)
     for s in range(1, LONG + 1):
         for h in range(2):
             j = arrived(s - 1, h, True)
@@ -219,43 +287,51 @@
                 i = arrived(s - 1, h, False)
                 if s < SHORT:
                     go(along(s, h, False))
-        put(j, s)
+        put(j)
         if s <= SHORT:
-            put(i, LONG + s)
+            put(i)
 
     for cp in sends:
         cp.wait_send()
     for cp in outs:
         cp.wait()
-    gt_copy.wait()
 
 
 def shards(tokens, value_grad, value_weight, counts, chosen_rows, loss_scale):
-    n = chosen_rows.shape[1]
-    live = lax.broadcasted_iota(jnp.int32, (1, n), 1) < counts[0]
-    sel = jnp.pad(jnp.where(live, chosen_rows, -1), ((0, 7), (0, ROWS - n)), constant_values=-1)
     vmem = pl.BlockSpec(memory_space=pltpu.VMEM)
+    hbm, smem = pl.BlockSpec(memory_space=pltpu.HBM), pl.BlockSpec(memory_space=pltpu.SMEM)
     dma = pltpu.SemaphoreType.DMA
     scratch = [
+        pltpu.VMEM((ROWS, D), bf16),
+        pltpu.VMEM((ROWS, KV), bf16),
+        pltpu.VMEM((W, KV), bf16),
+        pltpu.VMEM((8, ROWS), jnp.int32),
         pltpu.VMEM((SLOTS, D), bf16),
         pltpu.VMEM((NF, SLOTS, KV), bf16),
         pltpu.VMEM((CH, NF, SLOTS, CW), bf16),
         pltpu.VMEM((NF, SLOTS, W), bf16),
         pltpu.VMEM((NF, SLOTS, W), bf16),
+        pltpu.VMEM((NY, W, LANE), f32),
+        pltpu.VMEM((CH, LONG, CW, LANE), bf16),
+        pltpu.VMEM((CH, SHORT, CW, LANE), bf16),
+        pltpu.VMEM((CH, LONG, CW, LANE), bf16),
+        pltpu.VMEM((CH, SHORT, CW, LANE), bf16),
+        pltpu.VMEM((NZ * ZR, LANE), f32),
+        pltpu.VMEM((NZ * ZR, LANE), bf16),
+        pltpu.VMEM((NZ - 1, ZR, LANE), bf16),
+        pltpu.VMEM((ZR, LANE), bf16),
+        pltpu.VMEM((NY, NZ * ZR, LANE), bf16),
+        pltpu.VMEM((NF, 8, LANE), f32),
+        pltpu.VMEM((NY, 8, LANE), f32),
+        pltpu.VMEM((NZ, 8, LANE), f32),
         pltpu.VMEM((ROWS, D), bf16),
         pltpu.VMEM((NY, W, LANE), f32),
-        pltpu.VMEM((CH, LONG, CW, LANE), f32),
-        pltpu.VMEM((CH, SHORT, CW, LANE), f32),
-        pltpu.VMEM((NZ * ZR, LANE), f32),
-        pltpu.VMEM((NZ - 1, ZR, LANE), f32),
-        pltpu.VMEM((ZR, LANE), f32),
-        pltpu.VMEM((NY, NZ * ZR, LANE), f32),
+        dma((3,)), dma((NY + 1,)), dma((NF - 1,)), dma((NF - 1,)), dma((NY - 1,)), dma((NY - 1,)), dma((NZ - 1,)), dma((NZ - 1,)),
         dma((3,)), dma((3,)), dma((4,)), dma((4,)),
         dma((CH, NF - 1)), dma((CH, NF - 1)), dma((NF - 1,)), dma((NF - 1,)),
         dma((CH, LONG)), dma((CH, LONG)), dma((CH, SHORT)), dma((CH, SHORT)),
         dma((NZ - 1,)), dma((NZ - 1,)), dma((NZ - 1,)), dma((NZ - 1,)),
         dma((LONG, 2)), dma((LONG, 2)), dma((SHORT, 2)), dma((SHORT, 2)),
-        dma((NY + 1,)),
     ]
     return pl.pallas_call(
         kernel,
@@ -263,13 +339,13 @@
             jax.ShapeDtypeStruct((ROWS, D), bf16),
             jax.ShapeDtypeStruct((W, KV), f32),
         ),
-        in_specs=[vmem] * 4 + [pl.BlockSpec(memory_space=pltpu.SMEM)],
-        out_specs=(pl.BlockSpec(memory_space=pl.ANY), pl.BlockSpec(memory_space=pl.ANY)),
+        in_specs=[hbm] * 3 + [smem, vmem, smem],
+        out_specs=(hbm, hbm),
         scratch_shapes=scratch,
         compiler_params=pltpu.CompilerParams(
-            collective_id=0, has_side_effects=True, vmem_limit_bytes=48 << 20
+            collective_id=0, has_side_effects=True, vmem_limit_bytes=60 << 20
         ),
-    )(tokens, value_grad, value_weight, sel, loss_scale)
+    )(tokens, value_grad, value_weight, counts, chosen_rows, loss_scale)
 
 
 def solution(mesh):

time: 115 us -> 98.8 us (0.86); the launches traced: 113 us -> 98.2 us
  Pallas kernels: 104 us -> 92.5 us
  local copies, waits for them, and re-layouts: 5.7 us -> 3.76 us
    pallas_call x1, Pallas kernels: 104 us -> 92.5 us  [shards(): pl.pallas_call(kernel, out_shape=(jax.ShapeDtypeStruct((ROWS, D), bf16),...]
    unnamed x8 -> x4, local copies, waits for them, and re-layouts: 5.69 us -> 3.76 us
where the time goes in v2:
time: 98.8 us; the launch traced here: 98.2 us
  Pallas kernels  92.5 us (94%)
  local copies, waits for them, and re-layouts  3.76 us (4%)
  between operations  1.94 us (2%)
    pallas_call x1, Pallas kernels, shards(): pl.pallas_call(kernel, out_shape=(jax.ShapeDtypeStruct((ROWS, D), bf16),...  92.5 us
    unnamed x4, local copies, waits for them, and re-layouts  3.76 us

profile of v2, /device:TPU:6, one launch (start us, length us, event | category | flops | bytes accessed | tf_op | source)
XLA Modules:
  0.0 98.2 jit_solution(9059161613053763477)
XLA Ops:
  1.9 92.5 %shard_map.77 = (bf16[128,4096]{1,0:T(8,128)(2,1)}, f32[512,1024]{1,0:T(8,128)}) custom-call(bf16[128,4096]{1,0:T(8,128)(2,1)} %tok_in.1, bf16[128,1024]{1,0:T(8,128)(2,1)} %vg_in.1, bf16[512,1024]{1,0:T(8,128)(2,1)} %wt_in.1, s32[1]{0:T(128)S(6)} %copy.10.count, s32[1,88]{1,0:T(1,128)} %chosen.1, f32[1]{0:T(128)S(6)} %copy.11.scale), custom_call_target="tpu_custom_call" | custom-call | tf_op jit(solution)/shard_map/pallas_call | solution.py:336
  94.4 0.0 copy-start
  94.4 2.4 %copy.12 = bf16[128,4096]{1,0:T(8,128)(2,1)} copy(bf16[128,4096]{1,0:T(8,128)(2,1)} %get-tuple-element.4) | data formatting | bytes 2097152
  96.8 0.0 copy-done
  96.8 1.3 %copy.13 = f32[512,1024]{1,0:T(8,128)} copy(f32[512,1024]{1,0:T(8,128)S(1)} %copy-done) | data formatting | bytes 4194304
Async XLA Ops:
  94.4 2.4 %copy-start = (f32[512,1024]{1,0:T(8,128)S(1)}, f32[512,1024]{1,0:T(8,128)}, u32[]{:S(2)}) copy-start(f32[512,1024]{1,0:T(8,128)} %get-tuple-element.5) | copy-start | bytes 6291460

commit v3 on v2

--- a/solution.py
+++ b/solution.py
@@ -112,9 +112,19 @@
 
     bounds(xb, xb_s, xb_r, [(dp, fdev(d)) for d in range(1, NF)])
 
-    for d in (1, 3, 2):
-        go(rcopy(cots.at[fs], cots.at[fs], cot_s.at[d - 1], cot_r.at[d - 1], (dp, xdev(d))))
-    go(rcopy(cots.at[fs], cots.at[fs], sib_s.at[0], sib_r.at[0], (dp, sib)))
+    fwd, back = xdev(sgn + 4), xdev(4 - sgn)
+    across = xdev(2)
+    mine = cots.at[fs]
+    go(rcopy(mine, mine, cot_s.at[0], cot_r.at[0], (dp, fwd)))
+    go(rcopy(mine, mine, cot_s.at[1], cot_r.at[1], (dp, back)))
+    go(rcopy(mine, mine, sib_s.at[0], sib_r.at[0], (dp, sib)))
+
+    def cot_in(i, frm):
+        ref = cots.at[frm]
+        rcopy(ref, ref, cot_s.at[i], cot_r.at[i], (dp, frm)).wait_recv()
+        if i == 0:
+            go(rcopy(ref, ref, cot_s.at[2], cot_r.at[2], (dp, fwd)))
+        go(rcopy(ref, ref, sib_s.at[i + 1], sib_r.at[i + 1], (dp, sib)))
 
     for k in range(CH):
         for d in (2, 6, 3, 7, 4, 5, 1):
@@ -123,17 +133,17 @@
             go(rcopy(picked.at[:, cols], parts.at[k, fs], pk_s.at[k, d - 1], pk_r.at[k, d - 1], (dp, to)))
         cols = pl.ds(pl.multiple_of(fs * W + k * CW, CW), CW)
         parts[k, fs] = picked[:, cols]
+        if k == 0:
+            cot_in(0, back)
 
     yb[0] = largest(xb, xb_s, xb_r)
     bounds(yb, yb_s, yb_r, [(ydev(d), fs) for d in range(1, NY)])
 
-    for d in (1, 3, 2):
-        frm = xdev(4 - d)
-        rcopy(cots.at[frm], cots.at[frm], cot_s.at[d - 1], cot_r.at[d - 1], (dp, frm)).wait_recv()
-        go(rcopy(cots.at[frm], cots.at[frm], sib_s.at[d], sib_r.at[d], (dp, sib)))
-    for d in range(4):
-        frm = lax.rem(x + 4 - d, 4) * 2 + 1 - c
-        rcopy(cots.at[frm], cots.at[frm], sib_s.at[d], sib_r.at[d], (dp, sib)).wait_recv()
+    cot_in(1, fwd)
+    cot_in(2, across)
+    for i, v in enumerate((0, sgn, -sgn, 2)):
+        ref = cots.at[lax.rem(x + v + 4, 4) * 2 + 1 - c]
+        rcopy(ref, ref, sib_s.at[i], sib_r.at[i], (dp, sib)).wait_recv()
 
     def steps(bound):
         a = TOP / jnp.maximum(bound[0:1], 1e-30)
@@ -193,11 +203,19 @@
             go(short_copy(k, s))
         if s == LONG:
             total = part[y, here] + value(rl[k, LONG - 1], y_i) + value(rs[k, SHORT - 1], y_i)
-            red[here] = total
-            ered[here] = code(total, z_a)
-
-    red[W:] = jnp.zeros((NZ * ZR - W, LANE), f32)
-    ered[W:] = jnp.zeros((NZ * ZR - W, LANE), bf16)
+            red[k, 0:CW] = total
+            ered[k, 0:CW] = code(total, z_a)
+            for r in range(3):
+                to = 3 * k + r
+                d = lax.rem(to - z + NZ, NZ)
+
+                @pl.when(to != z)
+                def _():
+                    src = ered.at[k, pl.ds(r * ZR, ZR)]
+                    rcopy(src, zrecv.at[d - 1], z_s.at[d - 1], z_r.at[d - 1], (y * NZ + to, fs)).start()
+
+    red[:, CW:] = jnp.zeros((CH, 3 * ZR - CW, LANE), f32)
+    ered[:, CW:] = jnp.ones((CH, 3 * ZR - CW, LANE), bf16)
 
     def slot_grads():
         for g in range(2):
@@ -209,88 +227,103 @@
             go(rcopy(slot.at[to], own.at[fs], sg_s.at[d - 1], sg_r.at[d - 1], (dp, to)))
         own[fs] = slot[fs]
 
-    product(0)
-    ins[2].wait()
-    slot_grads()
-    z_a, z_i = steps(largest(zb, zb_s, zb_r) * (NF * NY * NZ))
-    for t in range(1, CH + LONG):
+    def z_sum(k):
+        @pl.when(z // 3 == k)
+        def _():
+            part_z = pl.ds(pl.multiple_of(lax.rem(z, 3) * ZR, 16), ZR)
+            total = red[k, part_z]
+            for d in (1, 11, 2, 10, 3, 9, 4, 8, 5, 7, 6):
+                rcopy(zrecv.at[d - 1], zrecv.at[d - 1], z_s.at[d - 1], z_r.at[d - 1], (dp, fs)).wait_recv()
+                total += value(zrecv[d - 1], z_i)
+            zsum[...] = code(total, z_a)
+            for d in (6, 5, 7, 4, 8, 3, 9, 2, 10, 1, 11):
+                rcopy(zsum, full.at[y, k, part_z], az_s.at[d - 1], az_r.at[d - 1], (y * NZ + zdev(d), fs)).start()
+            full[y, k, part_z] = zsum[...]
+
+    def along(k, s, up):
+        ref = full.at[at_y(y - sgn * s) if up else at_y(y + sgn * s), k, pl.ds(0, CW)]
+        if up:
+            return rcopy(ref, ref, al_s.at[k, s], al_r.at[k, s], (y_up, fs))
+        return rcopy(ref, ref, as_s.at[k, s], as_r.at[k, s], (y_dn, fs))
+
+    def arrived(k, s, up):
+        j = at_y(y - sgn * (s + 1)) if up else at_y(y + sgn * (s + 1))
+        ref = full.at[j, k, pl.ds(0, CW)]
+        sems = (al_s.at[k, s], al_r.at[k, s]) if up else (as_s.at[k, s], as_r.at[k, s])
+        rcopy(ref, ref, *sems, (dp, fs)).wait_recv()
+        return j
+
+    def put(k, j):
+        gw[k * CW:(k + 1) * CW, pl.ds(pl.multiple_of(j * LANE, LANE), LANE)] = value(full[j, k, 0:CW], z_i / scale[0])
+
+    def z_in(k):
+        for r in range(3):
+            frm = 3 * k + r
+            d = lax.rem(z - frm + NZ, NZ)
+
+            @pl.when(frm != z)
+            def _():
+                ref = full.at[y, k, pl.ds(r * ZR, ZR)]
+                rcopy(ref, ref, az_s.at[d - 1], az_r.at[d - 1], (dp, fs)).wait_recv()
+        go(along(k, 0, True))
+        go(along(k, 0, False))
+        put(k, y)
+
+    outs = []
+
+    def out(src, dst, i):
+        cp = pltpu.make_async_copy(src, dst, out_s.at[i])
+        cp.start()
+        outs.append(cp)
+
+    def y_step(k, s):
+        js = [arrived(k, s - 1, True)]
+        if s < LONG:
+            go(along(k, s, True))
+        if s <= SHORT:
+            js.append(arrived(k, s - 1, False))
+            if s < SHORT:
+                go(along(k, s, False))
+        for j in js:
+            put(k, j)
+        if s == LONG:
+            here = pl.ds(k * CW, CW)
+            out(gw.at[here], gw_out.at[here], k)
+
+    def tokens_grad():
+        for d in range(1, NF):
+            frm = fdev(NF - d)
+            rcopy(own.at[frm], own.at[frm], sg_s.at[d - 1], sg_r.at[d - 1], (dp, frm)).wait_recv()
+        hot_s = hot[:, :SLOTS]
+        for f in range(NF):
+            gt[:, f * W:(f + 1) * W] = dot(hot_s, own[f], 1, 0).astype(bf16)
+        out(gt, gt_out, CH)
+
+    z_at = LONG + 3
+    in_at = z_at + 3
+    for t in range(CH + in_at + LONG):
+        for s in range(LONG, 0, -1):
+            if 0 <= t - in_at - s < CH:
+                y_step(t - in_at - s, s)
+        if 0 <= t - in_at < CH:
+            z_in(t - in_at)
+        if 0 <= t - z_at < CH:
+            z_sum(t - z_at)
         if t < CH:
             product(t)
-        for s in range(min(t, LONG), 0, -1):
-            k = t - s
-            if k < CH:
-                ring_step(k, s)
-
-    for d in (6, 5, 7, 4, 8, 3, 9, 2, 10, 1, 11):
-        to = zdev(d)
-        src = ered.at[pl.ds(pl.multiple_of(to * ZR, 16), ZR)]
-        go(rcopy(src, zrecv.at[d - 1], z_s.at[d - 1], z_r.at[d - 1], (y * NZ + to, fs)))
-
-    for d in range(1, NF):
-        frm = fdev(NF - d)
-        rcopy(own.at[frm], own.at[frm], sg_s.at[d - 1], sg_r.at[d - 1], (dp, frm)).wait_recv()
-    hot_s = hot[:, :SLOTS]
-    for f in range(NF):
-        gt[:, f * W:(f + 1) * W] = dot(hot_s, own[f], 1, 0).astype(bf16)
-
-    outs = [pltpu.make_async_copy(gt, gt_out, out_s.at[NY])]
-    outs[0].start()
-    total = red[pl.ds(pl.multiple_of(z * ZR, 16), ZR)]
+        for s in range(LONG, 0, -1):
+            if 0 <= t - s < CH:
+                ring_step(t - s, s)
+        if t == 1:
+            ins[2].wait()
+            slot_grads()
+            z_a, z_i = steps(largest(zb, zb_s, zb_r) * (NF * NY * NZ))
+        if t == CH + LONG:
+            tokens_grad()
+
     for d in range(1, NZ):
-        rcopy(zrecv.at[d - 1], zrecv.at[d - 1], z_s.at[d - 1], z_r.at[d - 1], (dp, fs)).wait_recv()
-        total += value(zrecv[d - 1], z_i)
-    zsum[...] = code(total, z_a)
-
-    mine = full.at[y, pl.ds(pl.multiple_of(z * ZR, 16), ZR)]
-    for d in (6, 5, 7, 4, 8, 3, 9, 2, 10, 1, 11):
-        go(rcopy(zsum, mine, az_s.at[d - 1], az_r.at[d - 1], (y * NZ + zdev(d), fs)))
-    mine[...] = zsum[...]
-    for d in range(1, NZ):
-        there = full.at[y, pl.ds(pl.multiple_of(zdev(NZ - d) * ZR, 16), ZR)]
-        rcopy(zsum, there, az_s.at[d - 1], az_r.at[d - 1], (dp, fs)).wait_recv()
-
-    out_i = z_i / scale[0]
-
-    def put(j):
-        i = len(outs) - 1
-        gw[i] = value(full[j, 0:W], out_i)
-        cp = pltpu.make_async_copy(gw.at[i], gw_out.at[:, pl.ds(pl.multiple_of(j * LANE, LANE), LANE)], out_s.at[i])
-        cp.start()
-        outs.append(cp)
-
-    half = W // 2
-
-    def along(s, h, up):
-        j = at_y(y - sgn * s) if up else at_y(y + sgn * s)
-        ref = full.at[j, pl.ds(h * half, half)]
-        if up:
-            return rcopy(ref, ref, al_s.at[s, h], al_r.at[s, h], (y_up, fs))
-        return rcopy(ref, ref, as_s.at[s, h], as_r.at[s, h], (y_dn, fs))
-
-    def arrived(s, h, up):
-        j = at_y(y - sgn * (s + 1)) if up else at_y(y + sgn * (s + 1))
-        ref = full.at[j, pl.ds(h * half, half)]
-        sems = (al_s.at[s, h], al_r.at[s, h]) if up else (as_s.at[s, h], as_r.at[s, h])
-        rcopy(ref, ref, *sems, (dp, fs)).wait_recv()
-        return j
-
-    for h in range(2):
-        go(along(0, h, True))
-        go(along(0, h, False))
-    put(y)
-    for s in range(1, LONG + 1):
-        for h in range(2):
-            j = arrived(s - 1, h, True)
-            if s < LONG:
-                go(along(s, h, True))
-            if s <= SHORT:
-                i = arrived(s - 1, h, False)
-                if s < SHORT:
-                    go(along(s, h, False))
-        put(j)
-        if s <= SHORT:
-            put(i)
-
+        rcopy(ered.at[0, pl.ds(0, ZR)], zrecv.at[d - 1], z_s.at[d - 1], z_r.at[d - 1], (dp, fs)).wait_send()
+        rcopy(zsum, zrecv.at[d - 1], az_s.at[d - 1], az_r.at[d - 1], (dp, fs)).wait_send()
     for cp in sends:
         cp.wait_send()
     for cp in outs:
@@ -316,22 +349,22 @@
         pltpu.VMEM((CH, SHORT, CW, LANE), bf16),
         pltpu.VMEM((CH, LONG, CW, LANE), bf16),
         pltpu.VMEM((CH, SHORT, CW, LANE), bf16),
-        pltpu.VMEM((NZ * ZR, LANE), f32),
-        pltpu.VMEM((NZ * ZR, LANE), bf16),
+        pltpu.VMEM((CH, 3 * ZR, LANE), f32),
+        pltpu.VMEM((CH, 3 * ZR, LANE), bf16),
         pltpu.VMEM((NZ - 1, ZR, LANE), bf16),
         pltpu.VMEM((ZR, LANE), bf16),
-        pltpu.VMEM((NY, NZ * ZR, LANE), bf16),
+        pltpu.VMEM((NY, CH, 3 * ZR, LANE), bf16),
         pltpu.VMEM((NF, 8, LANE), f32),
         pltpu.VMEM((NY, 8, LANE), f32),
         pltpu.VMEM((NZ, 8, LANE), f32),
         pltpu.VMEM((ROWS, D), bf16),
-        pltpu.VMEM((NY, W, LANE), f32),
-        dma((3,)), dma((NY + 1,)), dma((NF - 1,)), dma((NF - 1,)), dma((NY - 1,)), dma((NY - 1,)), dma((NZ - 1,)), dma((NZ - 1,)),
+        pltpu.VMEM((W, KV), f32),
+        dma((3,)), dma((CH + 1,)), dma((NF - 1,)), dma((NF - 1,)), dma((NY - 1,)), dma((NY - 1,)), dma((NZ - 1,)), dma((NZ - 1,)),
         dma((3,)), dma((3,)), dma((4,)), dma((4,)),
         dma((CH, NF - 1)), dma((CH, NF - 1)), dma((NF - 1,)), dma((NF - 1,)),
         dma((CH, LONG)), dma((CH, LONG)), dma((CH, SHORT)), dma((CH, SHORT)),
         dma((NZ - 1,)), dma((NZ - 1,)), dma((NZ - 1,)), dma((NZ - 1,)),
-        dma((LONG, 2)), dma((LONG, 2)), dma((SHORT, 2)), dma((SHORT, 2)),
+        dma((CH, LONG)), dma((CH, LONG)), dma((CH, SHORT)), dma((CH, SHORT)),
     ]
     return pl.pallas_call(
         kernel,

time: 98.8 us -> 96.6 us (0.978)
  the two profiles are of different devices: /device:TPU:6 before, /device:TPU:8 now
where the time goes in v3:
time: 96.6 us; the launch traced here: 96.4 us
  Pallas kernels  90.7 us (94%)
  local copies, waits for them, and re-layouts  3.76 us (4%)
  between operations  1.94 us (2%)
    pallas_call x1, Pallas kernels, shards(): pl.pallas_call(kernel, out_shape=(jax.ShapeDtypeStruct((ROWS, D), bf16),...  90.7 us
    unnamed x4, local copies, waits for them, and re-layouts  3.76 us

profile of v3, /device:TPU:8, one launch (start us, length us, event | category | flops | bytes accessed | tf_op | source)
XLA Modules:
  0.0 96.4 jit_solution(1151630002668364939)
XLA Ops:
  1.9 90.7 %shard_map.77 = (bf16[128,4096]{1,0:T(8,128)(2,1)}, f32[512,1024]{1,0:T(8,128)}) custom-call(bf16[128,4096]{1,0:T(8,128)(2,1)} %tok_in.1, bf16[128,1024]{1,0:T(8,128)(2,1)} %vg_in.1, bf16[512,1024]{1,0:T(8,128)(2,1)} %wt_in.1, s32[1]{0:T(128)S(6)} %copy.10.count, s32[1,88]{1,0:T(1,128)} %chosen.1, f32[1]{0:T(128)S(6)} %copy.11.scale), custom_call_target="tpu_custom_call" | custom-call | tf_op jit(solution)/shard_map/pallas_call | solution.py:369
  92.7 0.0 copy-start
  92.7 2.4 %copy.12 = bf16[128,4096]{1,0:T(8,128)(2,1)} copy(bf16[128,4096]{1,0:T(8,128)(2,1)} %get-tuple-element.4) | data formatting | bytes 2097152
  95.1 0.0 copy-done
  95.1 1.3 %copy.13 = f32[512,1024]{1,0:T(8,128)} copy(f32[512,1024]{1,0:T(8,128)S(1)} %copy-done) | data formatting | bytes 4194304
Async XLA Ops:
  92.7 2.4 %copy-start = (f32[512,1024]{1,0:T(8,128)S(1)}, f32[512,1024]{1,0:T(8,128)}, u32[]{:S(2)}) copy-start(f32[512,1024]{1,0:T(8,128)} %get-tuple-element.5) | copy-start | bytes 6291460

commit v4 on v3

--- a/solution.py
+++ b/solution.py
@@ -15,6 +15,7 @@
 ZR = 48
 LANE = KV // NY
 LONG, SHORT = NY // 2, NY // 2 - 1
+RS_DIRECT, AG_DIRECT = (), (3,)
 f32, bf16 = jnp.float32, jnp.bfloat16
 TOP, LOW = 2.0 ** 15.4, 2.0 ** -15.4
 
@@ -25,9 +26,9 @@
 
 def kernel(
     tok_in, vg_in, wt_in, count, chosen, scale, gt_out, gw_out,
-    tok, vg, wt, sel, picked, cots, parts, slot, own, part, el, es, rl, rs, red, ered, zrecv, zsum, full, xb, yb, zb,
-    gt, gw, in_s, out_s, xb_s, xb_r, yb_s, yb_r, zb_s, zb_r, cot_s, cot_r, sib_s, sib_r, pk_s, pk_r, sg_s, sg_r,
-    l_s, l_r, s_s, s_r, z_s, z_r, az_s, az_r, al_s, al_r, as_s, as_r,
+    tok, vg, wt, sel, picked, cots, parts, slot, own, part, el, es, ed, rl, rs, rd, red, ered, zrecv, zsum, full, xb, yb, zb,
+    in_s, xb_s, xb_r, yb_s, yb_r, zb_s, zb_r, cot_s, cot_r, sib_s, sib_r, pk_s, pk_r, sg_s, sg_r,
+    l_s, l_r, s_s, s_r, z_s, z_r, az_s, az_r, al_s, al_r, as_s, as_r, d_s, d_r, g_s, g_r,
 ):
     dp, fs = lax.axis_index("dp"), lax.axis_index("fsdp")
     y, z = dp // NZ, lax.rem(dp, NZ)
@@ -126,15 +127,17 @@
             go(rcopy(ref, ref, cot_s.at[2], cot_r.at[2], (dp, fwd)))
         go(rcopy(ref, ref, sib_s.at[i + 1], sib_r.at[i + 1], (dp, sib)))
 
-    for k in range(CH):
+    def picks(k):
         for d in (2, 6, 3, 7, 4, 5, 1):
             to = fdev(d)
             cols = pl.ds(pl.multiple_of(to * W + k * CW, CW), CW)
             go(rcopy(picked.at[:, cols], parts.at[k, fs], pk_s.at[k, d - 1], pk_r.at[k, d - 1], (dp, to)))
         cols = pl.ds(pl.multiple_of(fs * W + k * CW, CW), CW)
         parts[k, fs] = picked[:, cols]
-        if k == 0:
-            cot_in(0, back)
+
+    picks(0)
+    cot_in(0, back)
+    picks(1)
 
     yb[0] = largest(xb, xb_s, xb_r)
     bounds(yb, yb_s, yb_r, [(ydev(d), fs) for d in range(1, NY)])
@@ -175,23 +178,51 @@
         src = es.at[k, s]
         return rcopy(src, rs.at[k, s], s_s.at[k, s], s_r.at[k, s], (y_up, fs))
 
+    def direct_copy(k, d):
+        return rcopy(ed.at[k, d - 1], rd.at[k, d - 1], d_s.at[k, d - 1], d_r.at[k, d - 1], (ydev(d), fs))
+
     def product(k):
         for d in range(1, NF):
             frm = fdev(NF - d)
             rcopy(parts.at[k, frm], parts.at[k, frm], pk_s.at[k, d - 1], pk_r.at[k, d - 1], (dp, frm)).wait_recv()
+        if k + 2 < CH:
+            picks(k + 2)
         a = parts[k].reshape(NF * SLOTS, CW)
         b = cots[...].reshape(NF * SLOTS, KV)
         p = dot(a, b, 0, 0)
         for j in range(NY):
             part[j, k * CW:(k + 1) * CW] = p[:, j * LANE:(j + 1) * LANE]
         here = pl.ds(k * CW, CW)
+        if k in RS_DIRECT:
+            for d in (4, 3, 5, 2, 6, 1, 7):
+                ed[k, d - 1] = code(part[at_y(y + d), here], y_a)
+                go(direct_copy(k, d))
+            return
         el[k, 0] = code(part[at_y(y - sgn * LONG), here], y_a)
         go(long_copy(k, 0))
         es[k, 0] = code(part[at_y(y + sgn * SHORT), here], y_a)
         go(short_copy(k, 0))
 
+    def reduced(k, total):
+        red[k, 0:CW] = total
+        ered[k, 0:CW] = code(total, z_a)
+        for r in range(3):
+            to = 3 * k + r
+            d = lax.rem(to - z + NZ, NZ)
+
+            @pl.when(to != z)
+            def _():
+                src = ered.at[k, pl.ds(r * ZR, ZR)]
+                rcopy(src, zrecv.at[d - 1], z_s.at[d - 1], z_r.at[d - 1], (y * NZ + to, fs)).start()
+
     def ring_step(k, s):
         here = pl.ds(k * CW, CW)
+        if k in RS_DIRECT:
+            if s == LONG - 1:
+                for d in range(1, NY):
+                    direct_copy(k, d).wait_recv()
+                reduced(k, part[y, here] + jnp.sum(value(rd[k], y_i), axis=0))
+            return
         long_copy(k, s - 1).wait_recv()
         if s < LONG:
             el[k, s] = code(part[at_y(y - sgn * (LONG - s)), here] + value(rl[k, s - 1], y_i), y_a)
@@ -202,17 +233,7 @@
             es[k, s] = code(part[at_y(y + sgn * (SHORT - s)), here] + value(rs[k, s - 1], y_i), y_a)
             go(short_copy(k, s))
         if s == LONG:
-            total = part[y, here] + value(rl[k, LONG - 1], y_i) + value(rs[k, SHORT - 1], y_i)
-            red[k, 0:CW] = total
-            ered[k, 0:CW] = code(total, z_a)
-            for r in range(3):
-                to = 3 * k + r
-                d = lax.rem(to - z + NZ, NZ)
-
-                @pl.when(to != z)
-                def _():
-                    src = ered.at[k, pl.ds(r * ZR, ZR)]
-                    rcopy(src, zrecv.at[d - 1], z_s.at[d - 1], z_r.at[d - 1], (y * NZ + to, fs)).start()
+            reduced(k, part[y, here] + value(rl[k, LONG - 1], y_i) + value(rs[k, SHORT - 1], y_i))
 
     red[:, CW:] = jnp.zeros((CH, 3 * ZR - CW, LANE), f32)
     ered[:, CW:] = jnp.ones((CH, 3 * ZR - CW, LANE), bf16)
@@ -231,11 +252,9 @@
         @pl.when(z // 3 == k)
         def _():
             part_z = pl.ds(pl.multiple_of(lax.rem(z, 3) * ZR, 16), ZR)
-            total = red[k, part_z]
-            for d in (1, 11, 2, 10, 3, 9, 4, 8, 5, 7, 6):
+            for d in range(1, NZ):
                 rcopy(zrecv.at[d - 1], zrecv.at[d - 1], z_s.at[d - 1], z_r.at[d - 1], (dp, fs)).wait_recv()
-                total += value(zrecv[d - 1], z_i)
-            zsum[...] = code(total, z_a)
+            zsum[...] = code(red[k, part_z] + jnp.sum(value(zrecv[...], z_i), axis=0), z_a)
             for d in (6, 5, 7, 4, 8, 3, 9, 2, 10, 1, 11):
                 rcopy(zsum, full.at[y, k, part_z], az_s.at[d - 1], az_r.at[d - 1], (y * NZ + zdev(d), fs)).start()
             full[y, k, part_z] = zsum[...]
@@ -254,7 +273,11 @@
         return j
 
     def put(k, j):
-        gw[k * CW:(k + 1) * CW, pl.ds(pl.multiple_of(j * LANE, LANE), LANE)] = value(full[j, k, 0:CW], z_i / scale[0])
+        gw_out[k * CW:(k + 1) * CW, pl.ds(pl.multiple_of(j * LANE, LANE), LANE)] = value(full[j, k, 0:CW], z_i / scale[0])
+
+    def gather_copy(k, j, d):
+        ref = full.at[j, k, pl.ds(0, CW)]
+        return rcopy(ref, ref, g_s.at[k, d - 1], g_r.at[k, d - 1], (ydev(d), fs))
 
     def z_in(k):
         for r in range(3):
@@ -265,18 +288,22 @@
             def _():
                 ref = full.at[y, k, pl.ds(r * ZR, ZR)]
                 rcopy(ref, ref, az_s.at[d - 1], az_r.at[d - 1], (dp, fs)).wait_recv()
-        go(along(k, 0, True))
-        go(along(k, 0, False))
+        if k in AG_DIRECT:
+            for d in (4, 3, 5, 2, 6, 1, 7):
+                go(gather_copy(k, y, d))
+        else:
+            go(along(k, 0, True))
+            go(along(k, 0, False))
         put(k, y)
 
-    outs = []
-
-    def out(src, dst, i):
-        cp = pltpu.make_async_copy(src, dst, out_s.at[i])
-        cp.start()
-        outs.append(cp)
-
     def y_step(k, s):
+        if k in AG_DIRECT:
+            if s == LONG:
+                for d in (1, 7, 2, 6, 3, 5, 4):
+                    j = at_y(y - d)
+                    gather_copy(k, j, d).wait_recv()
+                    put(k, j)
+            return
         js = [arrived(k, s - 1, True)]
         if s < LONG:
             go(along(k, s, True))
@@ -286,9 +313,6 @@
                 go(along(k, s, False))
         for j in js:
             put(k, j)
-        if s == LONG:
-            here = pl.ds(k * CW, CW)
-            out(gw.at[here], gw_out.at[here], k)
 
     def tokens_grad():
         for d in range(1, NF):
@@ -296,29 +320,29 @@
             rcopy(own.at[frm], own.at[frm], sg_s.at[d - 1], sg_r.at[d - 1], (dp, frm)).wait_recv()
         hot_s = hot[:, :SLOTS]
         for f in range(NF):
-            gt[:, f * W:(f + 1) * W] = dot(hot_s, own[f], 1, 0).astype(bf16)
-        out(gt, gt_out, CH)
+            gt_out[:, f * W:(f + 1) * W] = dot(hot_s, own[f], 1, 0).astype(bf16)
 
     z_at = LONG + 3
     in_at = z_at + 3
     for t in range(CH + in_at + LONG):
-        for s in range(LONG, 0, -1):
+        if t < CH:
+            product(t)
+        for s in range(1, LONG + 1):
+            if 0 <= t - s < CH:
+                ring_step(t - s, s)
+        if 0 <= t - z_at < CH:
+            z_sum(t - z_at)
+        if 0 <= t - in_at < CH:
+            z_in(t - in_at)
+        for s in range(1, LONG + 1):
             if 0 <= t - in_at - s < CH:
                 y_step(t - in_at - s, s)
-        if 0 <= t - in_at < CH:
-            z_in(t - in_at)
-        if 0 <= t - z_at < CH:
-            z_sum(t - z_at)
-        if t < CH:
-            product(t)
-        for s in range(LONG, 0, -1):
-            if 0 <= t - s < CH:
-                ring_step(t - s, s)
-        if t == 1:
+        if t == CH - 1:
             ins[2].wait()
             slot_grads()
+        if t == 1:
             z_a, z_i = steps(largest(zb, zb_s, zb_r) * (NF * NY * NZ))
-        if t == CH + LONG:
+        if t == in_at + CH - 1:
             tokens_grad()
 
     for d in range(1, NZ):
@@ -326,9 +350,6 @@
         rcopy(zsum, zrecv.at[d - 1], az_s.at[d - 1], az_r.at[d - 1], (dp, fs)).wait_send()
     for cp in sends:
         cp.wait_send()
-    for cp in outs:
-        cp.wait()
-
 
 def shards(tokens, value_grad, value_weight, counts, chosen_rows, loss_scale):
     vmem = pl.BlockSpec(memory_space=pltpu.VMEM)
@@ -347,8 +368,10 @@
         pltpu.VMEM((NY, W, LANE), f32),
         pltpu.VMEM((CH, LONG, CW, LANE), bf16),
         pltpu.VMEM((CH, SHORT, CW, LANE), bf16),
+        pltpu.VMEM((CH, NY - 1, CW, LANE), bf16),
         pltpu.VMEM((CH, LONG, CW, LANE), bf16),
         pltpu.VMEM((CH, SHORT, CW, LANE), bf16),
+        pltpu.VMEM((CH, NY - 1, CW, LANE), bf16),
         pltpu.VMEM((CH, 3 * ZR, LANE), f32),
         pltpu.VMEM((CH, 3 * ZR, LANE), bf16),
         pltpu.VMEM((NZ - 1, ZR, LANE), bf16),
@@ -357,26 +380,25 @@
         pltpu.VMEM((NF, 8, LANE), f32),
         pltpu.VMEM((NY, 8, LANE), f32),
         pltpu.VMEM((NZ, 8, LANE), f32),
-        pltpu.VMEM((ROWS, D), bf16),
-        pltpu.VMEM((W, KV), f32),
-        dma((3,)), dma((CH + 1,)), dma((NF - 1,)), dma((NF - 1,)), dma((NY - 1,)), dma((NY - 1,)), dma((NZ - 1,)), dma((NZ - 1,)),
+        dma((3,)), dma((NF - 1,)), dma((NF - 1,)), dma((NY - 1,)), dma((NY - 1,)), dma((NZ - 1,)), dma((NZ - 1,)),
         dma((3,)), dma((3,)), dma((4,)), dma((4,)),
         dma((CH, NF - 1)), dma((CH, NF - 1)), dma((NF - 1,)), dma((NF - 1,)),
         dma((CH, LONG)), dma((CH, LONG)), dma((CH, SHORT)), dma((CH, SHORT)),
         dma((NZ - 1,)), dma((NZ - 1,)), dma((NZ - 1,)), dma((NZ - 1,)),
         dma((CH, LONG)), dma((CH, LONG)), dma((CH, SHORT)), dma((CH, SHORT)),
+        dma((CH, NY - 1)), dma((CH, NY - 1)), dma((CH, NY - 1)), dma((CH, NY - 1)),
     ]
     return pl.pallas_call(
         kernel,
         out_shape=(
-            jax.ShapeDtypeStruct((ROWS, D), bf16),
-            jax.ShapeDtypeStruct((W, KV), f32),
+            pltpu.VMEM((ROWS, D), bf16),
+            pltpu.VMEM((W, KV), f32),
         ),
         in_specs=[hbm] * 3 + [smem, vmem, smem],
-        out_specs=(hbm, hbm),
+        out_specs=(vmem, vmem),
         scratch_shapes=scratch,
         compiler_params=pltpu.CompilerParams(
-            collective_id=0, has_side_effects=True, vmem_limit_bytes=60 << 20
+            collective_id=0, has_side_effects=True, vmem_limit_bytes=56 << 20
         ),
     )(tokens, value_grad, value_weight, counts, chosen_rows, loss_scale)
 

time: 96.6 us -> 90 us (0.932)
  Pallas kernels: 90.7 us -> 85.6 us
  local copies, waits for them, and re-layouts: 3.76 us -> 2.29 us
    pallas_call x1, Pallas kernels: 90.7 us -> 85.6 us  [shards(): pl.pallas_call(kernel, out_shape=(pltpu.VMEM((ROWS, D), bf16), pltpu.VMEM...]
    unnamed x4 -> x2, local copies, waits for them, and re-layouts: 3.76 us -> 2.29 us
where the time goes in v4:
time: 90 us; the launch traced here: 89.8 us
  Pallas kernels  85.6 us (95%)
  local copies, waits for them, and re-layouts  2.29 us (3%)
  between operations  1.93 us (2%)
    pallas_call x1, Pallas kernels, shards(): pl.pallas_call(kernel, out_shape=(pltpu.VMEM((ROWS, D), bf16), pltpu.VMEM...  85.6 us
    unnamed x2, local copies, waits for them, and re-layouts  2.29 us

profile of v4, /device:TPU:8, one launch (start us, length us, event | category | flops | bytes accessed | tf_op | source)
XLA Modules:
  0.0 89.8 jit_solution(9731814269153405114)
XLA Ops:
  1.9 85.6 %shard_map.77 = (bf16[128,4096]{1,0:T(8,128)(2,1)S(1)}, f32[512,1024]{1,0:T(8,128)S(1)}) custom-call(bf16[128,4096]{1,0:T(8,128)(2,1)} %tok_in.1, bf16[128,1024]{1,0:T(8,128)(2,1)} %vg_in.1, bf16[512,1024]{1,0:T(8,128)(2,1)} %wt_in.1, s32[1]{0:T(128)S(6)} %copy.12.count, s32[1,88]{1,0:T(1,128)} %chosen.1, f32[1]{0:T(128)S(6)} %copy.13.scale), custom_call_target="tpu_custom_call" | custom-call | tf_op jit(solution)/shard_map/pallas_call | solution.py:391
  87.5 1.0 %copy.10 = bf16[128,4096]{1,0:T(8,128)(2,1)} copy(bf16[128,4096]{1,0:T(8,128)(2,1)S(1)} %get-tuple-element.2) | data formatting | bytes 2097152
  88.5 1.3 %copy.11 = f32[512,1024]{1,0:T(8,128)} copy(f32[512,1024]{1,0:T(8,128)S(1)} %get-tuple-element.3) | data formatting | bytes 4194304

commit v5 on v4

--- a/solution.py
+++ b/solution.py
@@ -135,15 +135,15 @@
         cols = pl.ds(pl.multiple_of(fs * W + k * CW, CW), CW)
         parts[k, fs] = picked[:, cols]
 
+    cot_in(0, back)
     picks(0)
-    cot_in(0, back)
-    picks(1)
 
     yb[0] = largest(xb, xb_s, xb_r)
     bounds(yb, yb_s, yb_r, [(ydev(d), fs) for d in range(1, NY)])
 
     cot_in(1, fwd)
     cot_in(2, across)
+    picks(1)
     for i, v in enumerate((0, sgn, -sgn, 2)):
         ref = cots.at[lax.rem(x + v + 4, 4) * 2 + 1 - c]
         rcopy(ref, ref, sib_s.at[i], sib_r.at[i], (dp, sib)).wait_recv()

time: 90 us -> 89 us (0.989)
  the two profiles are of different devices: /device:TPU:8 before, /device:TPU:6 now
where the time goes in v5:
time: 89 us; the launch traced here: 88.8 us
  Pallas kernels  84.6 us (95%)
  local copies, waits for them, and re-layouts  2.29 us (3%)
  between operations  1.93 us (2%)
    pallas_call x1, Pallas kernels, shards(): pl.pallas_call(kernel, out_shape=(pltpu.VMEM((ROWS, D), bf16), pltpu.VMEM...  84.6 us
    unnamed x2, local copies, waits for them, and re-layouts  2.29 us

profile of v5, /device:TPU:6, one launch (start us, length us, event | category | flops | bytes accessed | tf_op | source)
XLA Modules:
  0.0 88.8 jit_solution(1579028106937374723)
XLA Ops:
  1.9 84.6 %shard_map.77 = (bf16[128,4096]{1,0:T(8,128)(2,1)S(1)}, f32[512,1024]{1,0:T(8,128)S(1)}) custom-call(bf16[128,4096]{1,0:T(8,128)(2,1)} %tok_in.1, bf16[128,1024]{1,0:T(8,128)(2,1)} %vg_in.1, bf16[512,1024]{1,0:T(8,128)(2,1)} %wt_in.1, s32[1]{0:T(128)S(6)} %copy.12.count, s32[1,88]{1,0:T(1,128)} %chosen.1, f32[1]{0:T(128)S(6)} %copy.13.scale), custom_call_target="tpu_custom_call" | custom-call | tf_op jit(solution)/shard_map/pallas_call | solution.py:391
  86.5 1.0 %copy.10 = bf16[128,4096]{1,0:T(8,128)(2,1)} copy(bf16[128,4096]{1,0:T(8,128)(2,1)S(1)} %get-tuple-element.2) | data formatting | bytes 2097152
  87.5 1.3 %copy.11 = f32[512,1024]{1,0:T(8,128)} copy(f32[512,1024]{1,0:T(8,128)S(1)} %get-tuple-element.3) | data formatting | bytes 4194304

commit v6 on v5

--- a/solution.py
+++ b/solution.py
@@ -128,7 +128,7 @@
         go(rcopy(ref, ref, sib_s.at[i + 1], sib_r.at[i + 1], (dp, sib)))
 
     def picks(k):
-        for d in (2, 6, 3, 7, 4, 5, 1):
+        for d in (4, 3, 5, 2, 6, 1, 7):
             to = fdev(d)
             cols = pl.ds(pl.multiple_of(to * W + k * CW, CW), CW)
             go(rcopy(picked.at[:, cols], parts.at[k, fs], pk_s.at[k, d - 1], pk_r.at[k, d - 1], (dp, to)))
@@ -243,7 +243,7 @@
             b = cots[g * 4:(g + 1) * 4].reshape(4 * SLOTS, KV)
             q = dot(b, wt[...], 1, 1).astype(bf16)
             slot[g * 4:(g + 1) * 4] = q.reshape(4, SLOTS, W)
-        for d in (2, 6, 3, 7, 4, 5, 1):
+        for d in (4, 3, 5, 2, 6, 1, 7):
             to = fdev(d)
             go(rcopy(slot.at[to], own.at[fs], sg_s.at[d - 1], sg_r.at[d - 1], (dp, to)))
         own[fs] = slot[fs]

time: 89 us -> 88.9 us (level); the launches traced: 88.8 us -> 87.4 us
  Pallas kernels: 84.6 us -> 83.2 us
    pallas_call x1, Pallas kernels: 84.6 us -> 83.2 us  [shards(): pl.pallas_call(kernel, out_shape=(pltpu.VMEM((ROWS, D), bf16), pltpu.VMEM...]
where the time goes in v6:
time: 88.9 us; the launch traced here: 87.4 us
  Pallas kernels  83.2 us (94%)
  local copies, waits for them, and re-layouts  2.29 us (3%)
  between operations  1.93 us (2%)
    pallas_call x1, Pallas kernels, shards(): pl.pallas_call(kernel, out_shape=(pltpu.VMEM((ROWS, D), bf16), pltpu.VMEM...  83.2 us
    unnamed x2, local copies, waits for them, and re-layouts  2.29 us

profile of v6, /device:TPU:6, one launch (start us, length us, event | category | flops | bytes accessed | tf_op | source)
XLA Modules:
  0.0 87.4 jit_solution(2189905517271614057)
XLA Ops:
  1.9 83.2 %shard_map.77 = (bf16[128,4096]{1,0:T(8,128)(2,1)S(1)}, f32[512,1024]{1,0:T(8,128)S(1)}) custom-call(bf16[128,4096]{1,0:T(8,128)(2,1)} %tok_in.1, bf16[128,1024]{1,0:T(8,128)(2,1)} %vg_in.1, bf16[512,1024]{1,0:T(8,128)(2,1)} %wt_in.1, s32[1]{0:T(128)S(6)} %copy.12.count, s32[1,88]{1,0:T(1,128)} %chosen.1, f32[1]{0:T(128)S(6)} %copy.13.scale), custom_call_target="tpu_custom_call" | custom-call | tf_op jit(solution)/shard_map/pallas_call | solution.py:391
  85.1 1.0 %copy.10 = bf16[128,4096]{1,0:T(8,128)(2,1)} copy(bf16[128,4096]{1,0:T(8,128)(2,1)S(1)} %get-tuple-element.2) | data formatting | bytes 2097152
  86.1 1.3 %copy.11 = f32[512,1024]{1,0:T(8,128)} copy(f32[512,1024]{1,0:T(8,128)S(1)} %get-tuple-element.3) | data formatting | bytes 4194304
